TPU v7x, 128 devices: a whole 4x4x4 slice. The times are simulated.
128 devices in a mesh: dp: 8 (over z, y_lo), mp: 16 (over y_hi, x, core).
Axes of the slice: x: 4, y: 4 (y_hi: 2, y_lo: 2; y = y_hi * 2 + y_lo), z: 4, core: 2. Of those that a mesh axis runs over, the one named last changes fastest.
Arguments:
- tokens: bfloat16 [1024, 8192], P(('dp', 'mp')), may hold values from -6 to 6
- out_grad: bfloat16 [1024, 8192], P(('dp', 'mp')), may hold values from -6 to 6
- gate_pre: bfloat16 [1024, 24576], P(None, 'mp'), may hold values from -8 to 8
- up_pre: bfloat16 [1024, 24576], P(None, 'mp'), may hold values from -6 to 6
- gate_weight: bfloat16 [8192, 24576], P('dp', 'mp'), may hold values from -0.0625 to 0.0625
- up_weight: bfloat16 [8192, 24576], P('dp', 'mp'), may hold values from -0.0625 to 0.0625
- down_weight: bfloat16 [24576, 8192], P('mp', 'dp'), may hold values from -0.0390625 to 0.0390625
- lengths: int32 [8], P('dp'), may hold values from 1 to 128, as said below
Outputs:
- grad_tokens: bfloat16 [1024, 8192], P(('dp', 'mp'))
- grad_gate: bfloat16 [8192, 24576], P('dp', 'mp')
- grad_up: bfloat16 [8192, 24576], P('dp', 'mp')
- grad_down: bfloat16 [24576, 8192], P('mp', 'dp')
Inputs may be any that keep to these rules, and one draw needn't show every extreme that they name: lengths count live rows from the start of each response's block of 128 rows; some response fills its block.
All inputs are finite; a program needn't handle non-finite values.
Results may differ from a plain program's by a relative error of at most 0.0051.
Values may be sent and summed in bfloat16 or wider, within the bound.
A program may use at most 128 MiB of HBM per device.

v0:
```python
import jax
import jax.numpy as jnp
from jax import lax
from jax.sharding import PartitionSpec as P

SEQ_LEN = 128


def gate_backward(dh, gate_f, up_f):
    sig = jax.nn.sigmoid(gate_f)
    dgate = (dh * up_f * sig * (1.0 + gate_f * (1.0 - sig))).astype(jnp.bfloat16)
    dup = (dh * gate_f * sig).astype(jnp.bfloat16)
    return (dgate, dup)


def local(tokens, out_grad, gate_pre, up_pre, gate_weight, up_weight, down_weight, lengths):
    own_rows = tokens.shape[0]
    position = lax.axis_index("mp") * own_rows + jnp.arange(own_rows, dtype=jnp.int32)
    which = position // SEQ_LEN
    table = which[:, None] == jnp.arange(lengths.shape[0], dtype=jnp.int32)[None, :]
    row_len = jnp.sum(jnp.where(table, lengths[None, :], 0), axis=1)
    live = position % SEQ_LEN < row_len
    masked = jnp.where(live[:, None], out_grad, jnp.zeros_like(out_grad))
    block_x, block_dy = (
        lax.all_gather(tokens, "mp", axis=0, tiled=True),
        lax.all_gather(masked, "mp", axis=0, tiled=True),
    )
    x_cols, dy_cols = (
        lax.all_to_all(block_x, "dp", split_axis=1, concat_axis=0, tiled=True),
        lax.all_to_all(block_dy, "dp", split_axis=1, concat_axis=0, tiled=True),
    )
    gate_f = gate_pre.astype(jnp.float32)
    up_f = up_pre.astype(jnp.float32)
    hidden = (gate_f * jax.nn.sigmoid(gate_f) * up_f).astype(jnp.bfloat16)
    term = jnp.einsum("td,fd->tf", dy_cols, down_weight, preferred_element_type=jnp.float32)
    dh = lax.psum(term, "dp")
    dgate, dup = gate_backward(dh, gate_f, up_f)
    grad_gate = jnp.einsum("td,tf->df", x_cols, dgate, preferred_element_type=jnp.float32).astype(
        jnp.bfloat16
    )
    grad_up = jnp.einsum("td,tf->df", x_cols, dup, preferred_element_type=jnp.float32).astype(
        jnp.bfloat16
    )
    grad_down = jnp.einsum("tf,td->fd", hidden, dy_cols, preferred_element_type=jnp.float32).astype(
        jnp.bfloat16
    )
    part_gate = jnp.einsum("tf,df->td", dgate, gate_weight, preferred_element_type=jnp.float32)
    part_up = jnp.einsum("tf,df->td", dup, up_weight, preferred_element_type=jnp.float32)
    moved = lax.all_to_all(part_gate + part_up, "dp", split_axis=0, concat_axis=1, tiled=True)
    grad_tokens = lax.psum_scatter(moved, "mp", scatter_dimension=0, tiled=True).astype(
        jnp.bfloat16
    )
    return (grad_tokens, grad_gate, grad_up, grad_down)


def solution(mesh):
    in_specs = (
        P(("dp", "mp"), None),
        P(("dp", "mp"), None),
        P(None, "mp"),
        P(None, "mp"),
        P("dp", "mp"),
        P("dp", "mp"),
        P("mp", "dp"),
        P("dp"),
    )
    out_specs = (P(("dp", "mp"), None), P("dp", "mp"), P("dp", "mp"), P("mp", "dp"))
    return jax.shard_map(local, mesh=mesh, in_specs=in_specs, out_specs=out_specs, check_vma=False)
```

profile of v0, /device:TPU:0, one launch (start us, length us, event | category | flops | bytes accessed | tf_op | source)
XLA Modules:
  0.0 531.1 jit_solution(5219921774945257977)
XLA Ops:
  7.2 0.0 all-gather.3.cloned.1.call-start
  8.0 1.7 broadcast_select_fusion
  9.8 0.0 all-gather.3.cloned.1.call-update
  9.8 0.0 all-reduce.2.cloned.1.call-start
  9.8 52.0 %all-gather.3.cloned.1.call-done = bf16[128,8192]{1,0:T(8,128)(2,1)} async-done(((bf16[8,8192]{1,0:T(8,128)(2,1)}), bf16[128,8192]{1,0:T(8,128)(2,1)}) %all-gather.3.cloned.1.call-update) | async-done | bytes 2097168 | tf_op jit(solution)/shard_map/all_gather | solution.py:26
  61.9 4.1 copy.25
  65.9 32.0 %all_to_all.57 = bf16[128,8,1024]{0,2,1:T(8,128)(2,1)} all-to-all(bf16[128,8,1024]{0,2,1:T(8,128)(2,1)} %bitcast.29), channel_id=1, replica_groups=mesh['dp'=8,'mp'=16] {'dp'}, dimensions={1} | all-to-all | bytes 4194304 | tf_op jit(solution)/shard_map/all_to_all | solution.py:30
  97.9 3.9 copy.26
  101.8 7.0 %fusion.15 = f32[1024,1536]{1,0:T(8,128)} fusion(bf16[1024,1024]{1,0:T(8,128)(2,1)} %bitcast.34, bf16[1536,1024]{1,0:T(8,128)(2,1)S(1)} %copy-done), kind=kOutput, calls=%fused_computation.31 | convolution fusion | flops 3221225472 | bytes 11534336 | tf_op jit(solution)/shard_map/td,fd->tf/dot_general | solution.py:35
  108.8 0.0 all-reduce.2.cloned.1.call-update
  108.8 0.0 all-gather.5.cloned.1.call-start
  108.9 0.7 all-gather.5.cloned.1.call-update
  109.6 0.0 reduce-scatter.2.cloned.1.call-start
  109.6 258.2 %all-reduce.2.cloned.1.call-done = f32[1024,1536]{1,0:T(8,128)} async-done(((f32[1024,1536]{1,0:T(8,128)}), f32[1024,1536]{1,0:T(8,128)}) %all-reduce.2.cloned.1.call-update) | async-done | bytes 6291472 | tf_op jit(solution)/shard_map/psum | solution.py:36
  367.8 5.6 %fusion.9 = (bf16[1024,1536]{1,0:T(8,128)(2,1)S(1)}, bf16[1024,1536]{1,0:T(8,128)(2,1)S(1)}) fusion(f32[1024,1536]{1,0:T(8,128)} %all-reduce.2.cloned.1.call-done, bf16[1024,1536]{1,0:T(8,128)(2,1)S(1)} %copy-done.2, bf16[1024,1536]{1,0:T(8,128)(2,1)} %param.11), kind=kLoop, calls=%fused_computation.15 | loop fusion | flops 23592960 | bytes 18874368 | tf_op jit(solution)/shard_map/convert_element_type | solution.py:12
  373.4 3.4 fusion.16
  376.9 0.7 copy-done.9
  377.6 3.5 convolution_add_fusion
  381.1 59.8 %all_to_all.58 = f32[8,128,1024]{2,1,0:T(8,128)S(1)} all-to-all(f32[8,128,1024]{2,1,0:T(8,128)S(1)} %bitcast.33), channel_id=1, replica_groups=mesh['dp'=8,'mp'=16] {'dp'}, dimensions={0} | all-to-all | bytes 8388608 | tf_op jit(solution)/shard_map/all_to_all | solution.py:49
  440.9 2.3 copy.32
  443.1 0.0 reduce-scatter.2.cloned.1.call-update
  443.2 0.0 all-gather.5.cloned.1.call-done
  443.2 3.2 copy.28
  446.4 29.2 %all_to_all.59 = bf16[128,8,1024]{0,2,1:T(8,128)(2,1)} all-to-all(bf16[128,8,1024]{0,2,1:T(8,128)(2,1)S(1)} %bitcast.31), channel_id=1, replica_groups=mesh['dp'=8,'mp'=16] {'dp'}, dimensions={1} | all-to-all | bytes 4194304 | tf_op jit(solution)/shard_map/all_to_all | solution.py:29
  475.6 4.6 copy.29
  480.2 8.4 %convolution_convert_fusion = bf16[1536,1024]{1,0:T(8,128)(2,1)} fusion(bf16[1024,1024]{1,0:T(8,128)(2,1)} %bitcast.35, bf16[1024,1536]{1,0:T(8,128)(2,1)} %param.11, bf16[1024,1536]{1,0:T(8,128)(2,1)S(1)} %copy-done.3), kind=kOutput, calls=%fused_computation.16 | convolution fusion | flops 3235381248 | bytes 11534336 | tf_op jit(solution)/shard_map/tf,td->fd/dot_general | solution.py:44
  488.7 3.7 fusion.10
  492.4 2.9 copy.30
  495.3 7.9 %fusion.11 = bf16[1024,1536]{0,1:T(8,128)(2,1)} fusion(bf16[1024,1536]{1,0:T(8,128)(2,1)} %copy-done.4, bf16[1024,1024]{1,0:T(8,128)(2,1)} %bitcast.36), kind=kOutput, calls=%fused_computation.20 | convolution fusion | flops 3222798336 | bytes 8388608 | tf_op jit(solution)/shard_map/td,tf->df/dot_general | solution.py:41
  503.2 4.6 copy.31
  507.8 15.1 %reduce-scatter.2.cloned.1.call-done = f32[8,8192]{1,0:T(8,128)} async-done(((f32[128,8192]{1,0:T(8,128)}), f32[8,8192]{1,0:T(8,128)}) %reduce-scatter.2.cloned.1.call-update) | async-done | bytes 262160 | tf_op jit(solution)/shard_map/reduce_scatter | solution.py:50
  522.9 1.6 convert_element_type.37
  (20 shorter events, 0.1 us)
Async XLA Ops:
  7.2 94.6 %copy-start = (bf16[1536,1024]{1,0:T(8,128)(2,1)S(1)}, bf16[1536,1024]{1,0:T(8,128)(2,1)}, u32[]{:S(2)}) copy-start(bf16[1536,1024]{1,0:T(8,128)(2,1)} %param.14) | copy-start | bytes 9437188
  7.2 54.7 %all-gather.3.cloned.1.call-start = ((), (), s32[]{:S(2)}) async-start(), calls=%async_computation.4 | async-start | bytes 2228224 | tf_op jit(solution)/shard_map/all_gather | solution.py:26
  9.8 358.0 %all-reduce.2.cloned.1.call-start = ((), (), s32[]{:S(2)}) async-start(), calls=%async_computation.5 | async-start | bytes 12582912 | tf_op jit(solution)/shard_map/psum | solution.py:36
  108.8 259.0 %copy-start.2 = (bf16[1024,1536]{1,0:T(8,128)(2,1)S(1)}, bf16[1024,1536]{1,0:T(8,128)(2,1)}, u32[]{:S(2)}) copy-start(bf16[1024,1536]{1,0:T(8,128)(2,1)} %param.10) | copy-start | bytes 9437188
  108.8 334.4 %all-gather.5.cloned.1.call-start = ((), (), s32[]{:S(2)}) async-start(), calls=%async_computation.7 | async-start | bytes 2228224 | tf_op jit(solution)/shard_map/all_gather | solution.py:25
  109.6 413.4 %reduce-scatter.2.cloned.1.call-start = ((), (), s32[]{:S(2)}) async-start(), calls=%async_computation.6 | async-start | bytes 4456448 | tf_op jit(solution)/shard_map/reduce_scatter | solution.py:50
  367.8 5.6 %copy-start.8 = (bf16[1024,1536]{1,0:T(8,128)(2,1)S(1)}, bf16[1024,1536]{1,0:T(8,128)(2,1)}, u32[]{:S(2)}) copy-start(bf16[1024,1536]{1,0:T(8,128)(2,1)} %param.12) | copy-start | bytes 9437188
  373.4 3.5 copy-start.5
  373.4 3.5 copy-start.4
  373.4 4.2 copy-start.9
  475.6 4.6 copy-start.3
  480.2 8.4 %copy-start.6 = (bf16[1024,1536]{1,0:T(8,128)(2,1)S(1)}, bf16[1024,1536]{1,0:T(8,128)(2,1)}, u32[]{:S(2)}) copy-start(bf16[1024,1536]{1,0:T(8,128)(2,1)} %copy-done.5) | copy-start | bytes 9437188
  480.2 8.4 %copy-start.7 = (bf16[8,128,1024]{2,1,0:T(8,128)(2,1)S(1)}, bf16[8,128,1024]{2,1,0:T(8,128)(2,1)}, u32[]{:S(2)}) copy-start(bf16[8,128,1024]{2,1,0:T(8,128)(2,1)} %copy.29) | copy-start | bytes 6291460
  495.3 29.2 %copy-start.1 = (bf16[1536,1024]{1,0:T(8,128)(2,1)S(1)}, bf16[1536,1024]{1,0:T(8,128)(2,1)}, u32[]{:S(2)}) copy-start(bf16[1536,1024]{1,0:T(8,128)(2,1)} %param.14) | copy-start | bytes 9437188
Sparse Core Ops, SparseCore 0:
  11.0 50.7 all-gather.2
  108.9 258.8 all-reduce.1
  370.2 54.5 all-gather.4
  443.3 79.5 reduce-scatter.1
where the time goes:
time: 532 us; the launch traced here: 531 us
  waiting for transfers between devices  326 us (61%)
  blocking collectives  121 us (23%)
  matrix products  33.9 us (6%)
  local copies, waits for them, and re-layouts  26.4 us (5%)
  between operations  14.7 us (3%)
  other arithmetic  8.96 us (2%)
    psum x1, waiting for transfers between devices, local(): dh = lax.psum(term, 'dp')  258 us
    all_to_all x1, blocking collectives, local(): lax.all_to_all(part_gate + part_up, 'dp', split_axis=0, concat_axis=1, ti...  59.8 us
    all_gather x1, waiting for transfers between devices, local(): lax.all_gather(masked, 'mp', axis=0, tiled=True)  52 us
    all_to_all x1, blocking collectives, local(): lax.all_to_all(block_dy, 'dp', split_axis=1, concat_axis=0, tiled=True)  32 us
    all_to_all x1, blocking collectives, local(): lax.all_to_all(block_x, 'dp', split_axis=1, concat_axis=0, tiled=True)  29.2 us
    reduce_scatter x1, waiting for transfers between devices, local(): lax.psum_scatter(moved, 'mp', scatter_dimension=0, tiled=True)  15.1 us
  transfers between devices with their start and end apart: 4, of which 3 were waited for; matrix products, arithmetic and copies ran while one was open for 9% of the time, Pallas kernels for 0%

commit v1 on v0

v1 whole, which is shorter than its diff:
```python
import functools

import jax
import jax.numpy as jnp
from jax import lax
from jax.experimental import pallas as pl
from jax.experimental.pallas import tpu as pltpu
from jax.sharding import PartitionSpec as P

SEQ_LEN = 128
NZ, NY = 4, 2
NF = 2
ND = 2
SIZE = 640
BF, F32 = jnp.bfloat16, jnp.float32
MIB = 1 << 20

TREE = (
    ((2, 1), (2, 0)),
    ((1, 1), (0, 1)),
    ((3, 1), (0, 1)),
    ((3, 0), (0, 0)),
    ((2, 0), (1, 0)),
    ((0, 1), (0, 0)),
    ((1, 0), (0, 0)),
)
FLAT = TREE[:4] + (((2, 0), (0, 0)),) + TREE[5:]


class Place:
    def __init__(self):
        self.dp = lax.axis_index("dp")
        self.mp = lax.axis_index("mp")
        self.z, self.yl = self.dp // NY, self.dp % NY
        self.core = self.mp % 2
        self.chip = self.mp // 2
        self.yh, self.x = self.chip // 4, self.chip % 4
        self.sign = 1 - 2 * self.core

    def dp_at(self, da, db):
        z = lax.rem(self.z + self.sign * da + 4, 4)
        return z * NY + (1 - self.yl if db else self.yl)

    def chip_at(self, da, db):
        x = lax.rem(self.x + self.sign * da + 4, 4)
        return (1 - self.yh if db else self.yh) * 4 + x

    def dp_hop(self, src, dst):
        return {"dp": self.dp_at(dst[0] - src[0], src[1] ^ dst[1])}

    def mp_hop(self, src, dst):
        return {"mp": self.chip_at(dst[0] - src[0], src[1] ^ dst[1]) * 2 + self.core}

    def sibling(self):
        return {"mp": self.chip * 2 + 1 - self.core}

    def greet(self):
        sem = pltpu.get_barrier_semaphore()
        peers = [{"dp": lax.rem(self.dp + k, 8)} for k in range(1, 8)]
        near = ((1, 0), (2, 0), (3, 0), (0, 1))
        peers += [self.sibling()]
        peers += [{"mp": self.chip_at(a, b) * 2 + self.core} for a, b in near]
        for peer in peers:
            pl.semaphore_signal(sem, inc=1, device_id=peer, device_id_type=pl.DeviceIdType.MESH)
        self.peers = len(peers)

    def meet(self):
        pl.semaphore_wait(pltpu.get_barrier_semaphore(), self.peers)


def remote(src, dst, send_sem, recv_sem, device):
    return pltpu.make_async_remote_copy(
        src_ref=src,
        dst_ref=dst,
        send_sem=send_sem,
        recv_sem=recv_sem,
        device_id=device,
        device_id_type=pl.DeviceIdType.MESH,
    )


def send(*args):
    copy = remote(*args)
    copy.start()
    return copy


def dot_nt(a, b):
    return lax.dot_general(a, b, (((1,), (1,)), ((), ())), preferred_element_type=F32)


def dot(a, b):
    return jnp.dot(a, b, preferred_element_type=F32)


class Gather:
    def __init__(self, at, buf, rows, sems):
        self.at, self.buf, self.rows = at, buf, rows
        self.send_sem, self.recv_sem, self.sib_send, self.sib_recv = sems
        self.copies = []

    def slab(self, chip, core):
        start = pl.multiple_of((core * 8 + chip) * self.rows, self.rows)
        return self.buf.at[pl.ds(start, self.rows), :]

    def slab_from(self, offset):
        return self.slab(self.at.chip_at(-offset[0], offset[1]), self.at.core)

    def put(self, value):
        start = pl.multiple_of((self.at.core * 8 + self.at.chip) * self.rows, self.rows)
        self.buf[pl.ds(start, self.rows), :] = value

    def hop(self, e):
        dst, src = FLAT[e]
        ref = self.slab_from(src)
        self.copies.append(
            send(ref, ref, self.send_sem.at[e], self.recv_sem.at[e], self.at.mp_hop(src, dst))
        )

    def to_sibling(self, n, offset):
        ref = self.slab_from(offset)
        self.copies.append(
            send(ref, ref, self.sib_send.at[n], self.sib_recv.at[n], self.at.sibling())
        )

    def arrive(self, e):
        offset = FLAT[e][0]
        arrival(self.slab_from(offset), self.send_sem.at[e], self.recv_sem.at[e], self.at)
        self.to_sibling(e, offset)

    def stage(self, n):
        if n == 0:
            for e in (5, 4, 6, 3):
                self.hop(e)
            self.to_sibling(7, (0, 0))
        elif n == 1:
            self.arrive(5)
            self.hop(1)
            self.hop(2)
            self.arrive(6)
            self.arrive(3)
        elif n == 2:
            self.arrive(4)
            self.hop(0)
        elif n == 3:
            for e in (1, 2, 0):
                self.arrive(e)
        else:
            for n, offset in enumerate([src for src, _ in FLAT] + [(0, 0)]):
                ref = self.slab(self.at.chip_at(*offset), 1 - self.at.core)
                arrival(ref, self.sib_send.at[n], self.sib_recv.at[n], self.at)

    def drain(self):
        for copy in self.copies:
            copy.wait_send()


def arrival(ref, send_sem, recv_sem, at):
    remote(ref, ref, send_sem, recv_sem, at.sibling()).wait_recv()


def live_rows(length, parity):
    rest = length & 15
    extra = jnp.where(parity == 0, jnp.minimum(rest, 8), jnp.maximum(rest - 8, 0))
    return (length >> 4) * 8 + extra


def rank_of(index, lens, h, slabs):
    if slabs:
        slab = index >> 5
        core = slab >> 3
        response = ((index >> 3) & 3) * 2 + ((core + h) & 1)
        place = ((slab & 7) * 2 + core) * 8 + (index & 7)
    else:
        response = index >> 7
        place = index & 127
    rank = jnp.full(index.shape, -1, jnp.int32)
    first = 0
    for r in range(8):
        parity = (r + h) & 1
        live = (response == r) & (place < lens[r]) & (((place >> 3) & 1) == parity)
        rank = jnp.where(live, (place >> 4) * 8 + (place & 7) + first, rank)
        first = first + live_rows(lens[r], parity)
    return rank


def fold(value):
    mid = value.shape[1] // 2
    return jnp.concatenate([value[:, :mid], value[:, mid:]], axis=0)


def main_kernel(
    tok_hbm,
    grad_hbm,
    length,
    gp,
    up,
    wg_hbm,
    wu_hbm,
    wd_hbm,
    gt_out,
    gg_out,
    gu_out,
    gd_out,
    over_out,
    tok,
    grad,
    sbuf,
    rbuf,
    dyb,
    xb,
    p_slab,
    p_own,
    p_back,
    dyc,
    wg,
    wu,
    wd,
    raw,
    act,
    hid,
    dact,
    term,
    rs_out,
    rs_in,
    dh,
    half_out,
    half_in,
    mp_out,
    mp_in,
    fin_out,
    fin_in,
    in_sem,
    a_send,
    a_recv,
    w_sem,
    raw_sem,
    out_sem,
    rs_send,
    rs_recv,
    ag_send,
    ag_recv,
    dy_send,
    dy_recv,
    dys_send,
    dys_recv,
    x_send,
    x_recv,
    xs_send,
    xs_recv,
    h_send,
    h_recv,
    m_send,
    m_recv,
    f_send,
    f_recv,
):
    at = Place()
    cap = dyc.shape[0] // 2
    rows = cap // 8
    fw = term.shape[3]
    dl = dyc.shape[1]
    dw = dl // ND
    sent = []

    loads = [
        pltpu.make_async_copy(src, dst, in_sem.at[n])
        for n, (src, dst) in enumerate(((tok_hbm, tok), (grad_hbm, grad)))
    ]
    for copy in loads:
        copy.start()
    at.greet()
    for copy in loads:
        copy.wait()
    own_len = jnp.full((16, 128), length[0], jnp.int32).astype(F32).astype(BF)
    for c in range(8):
        cols = slice(c * dl, (c + 1) * dl)
        both = jnp.concatenate([tok[:, cols].astype(F32), grad[:, cols].astype(F32)], axis=0)
        sbuf[c, :, :dl] = both.astype(BF)
        sbuf[c, :, dl:] = own_len
    at.meet()
    for k in (4, 3, 5, 2, 6, 1, 7):
        peer = lax.rem(at.dp + k, 8)
        sent.append(
            send(sbuf.at[peer], rbuf.at[at.dp], a_send.at[k], a_recv.at[k], {"dp": peer})
        )
    rbuf[at.dp] = sbuf[at.dp]

    def piece(j):
        return pl.ds(pl.multiple_of(j * fw, fw), fw)

    weights = [pltpu.make_async_copy(wd_hbm, wd, w_sem.at[0])]
    for j in range(NF):
        for n, (src, dst) in enumerate(((wg_hbm, wg), (wu_hbm, wu))):
            sem = w_sem.at[1 + 2 * j + n]
            weights.append(pltpu.make_async_copy(src.at[:, piece(j)], dst.at[j], sem))
    raws = [
        pltpu.make_async_copy(
            (gp, up)[n % 2].at[:, (n // 2) * fw : (n // 2 + 1) * fw], raw.at[n], raw_sem.at[n]
        )
        for n in range(2 * NF)
    ]
    weights[0].start()
    for copy in raws:
        copy.start()
    for k in (4, 3, 5, 2, 6, 1, 7):
        source = lax.rem(at.dp + 8 - k, 8)
        arrival(rbuf.at[source], a_send.at[k], a_recv.at[k], at)

    def slab_of(h, first):
        parity = (at.core + h) & 1
        blocks = [rbuf[2 * k + parity].astype(F32)[first : first + 8, :dl] for k in range(4)]
        return jnp.concatenate(blocks, axis=0).astype(BF)


    def one_hot(ref, slot, h, slabs):
        size = ref.shape[2]
        rank = rank_of(lax.broadcasted_iota(jnp.int32, (1, size), 1), lens, h, slabs)
        blk = 64

        @pl.loop(0, cap // blk)
        def _(i):
            start = pl.multiple_of(i * blk, blk)
            index = lax.broadcasted_iota(jnp.int32, (blk, size), 0) + start
            ref[slot, pl.ds(start, blk), :] = jnp.where(index == rank, 1.0, 0.0).astype(BF)

    def back_matrix(h):
        blk = 128

        @pl.loop(0, 512 // blk)
        def _(i):
            start = pl.multiple_of(i * blk, blk)
            index = lax.broadcasted_iota(jnp.int32, (blk, 1), 0) + start
            rank = rank_of(index, lens, h, True)
            lane = lax.broadcasted_iota(jnp.int32, (blk, cap), 1)
            p_back[pl.ds(start, blk), :] = jnp.where(lane == rank, 1.0, 0.0).astype(BF)

    gather_dy, gather_x = [], []
    for h in range(2):
        sems = [sem.at[h] for sem in (dy_send, dy_recv, dys_send, dys_recv)]
        gather_dy.append(Gather(at, dyb.at[h], 32, sems))
        gather_dy[h].put(slab_of(h, 8))
        gather_dy[h].stage(0)
    for h in range(2):
        sems = [sem.at[h] for sem in (x_send, x_recv, xs_send, xs_recv)]
        gather_x.append(Gather(at, xb.at[h], 32, sems))
        gather_x[h].put(slab_of(h, 0))
    lens = [jnp.max(rbuf[r].astype(F32)[0:1, dl:]).astype(jnp.int32) for r in range(8)]
    need = [sum(live_rows(lens[r], (r + h) & 1) for r in range(8)) for h in range(2)]
    over_out[0] = (jnp.maximum(need[0], need[1]) > cap).astype(jnp.int32)

    def half_rows(h):
        return slice(h * cap, (h + 1) * cap)

    def chunk(h, j, offset):
        owner = at.dp_at(-offset[0], offset[1])
        return fold(term[h, j, pl.ds(pl.multiple_of(owner * rows, rows), rows), :])

    def rs_copy(h, j, e):
        src, dst = TREE[e]
        return remote(
            rs_out.at[h, j, e],
            rs_in.at[h, j, e],
            rs_send.at[h, j, e],
            rs_recv.at[h, j, e],
            at.dp_hop(src, dst),
        )

    def rs_hop(h, j, e, value):
        rs_out[h, j, e] = value.astype(BF)
        rs_copy(h, j, e).start()

    def rs_arrive(h, j, e):
        arrival(rs_in.at[h, j, e], rs_send.at[h, j, e], rs_recv.at[h, j, e], at)
        return rs_in[h, j, e].astype(F32)

    def terms(h):
        dyc[half_rows(h), :] = dot(p_slab[h], dyb[h]).astype(BF)
        if h == 0:
            weights[0].wait()

        @pl.loop(0, NF)
        def _(j):
            term[h, j] = dot_nt(dyc[half_rows(h), :], wd[piece(j), :])
            for e in range(4):
                rs_hop(h, j, e, chunk(h, j, TREE[e][0]))

    def rs4(h):
        @pl.loop(0, NF)
        def _(j):
            rs_hop(h, j, 4, chunk(h, j, (2, 0)) + rs_arrive(h, j, 0))

    def rs5(h):
        @pl.loop(0, NF)
        def _(j):
            rs_hop(h, j, 5, chunk(h, j, (0, 1)) + rs_arrive(h, j, 1) + rs_arrive(h, j, 2))

    def rs6(h):
        @pl.loop(0, NF)
        def _(j):
            rs_hop(h, j, 6, chunk(h, j, (1, 0)) + rs_arrive(h, j, 4))

    def ag_ref(h, j, offset):
        return dh.at[h, j, at.dp_at(-offset[0], offset[1])]

    def ag_copy(h, j, e):
        dst, src = TREE[e]
        ref = ag_ref(h, j, src)
        return remote(ref, ref, ag_send.at[h, j, e], ag_recv.at[h, j, e], at.dp_hop(src, dst))

    def ag_hop(h, j, e):
        ag_copy(h, j, e).start()

    def ag_arrive(h, j, e):
        arrival(ag_ref(h, j, TREE[e][0]), ag_send.at[h, j, e], ag_recv.at[h, j, e], at)

    def rs_own(h):
        @pl.loop(0, NF)
        def _(j):
            value = chunk(h, j, (0, 0)) + rs_arrive(h, j, 3)
            value = value + rs_arrive(h, j, 5) + rs_arrive(h, j, 6)
            dh[h, j, at.dp] = value.astype(BF)
            for e in (6, 5, 3):
                ag_hop(h, j, e)

    def ag_forward(h):
        @pl.loop(0, NF)
        def _(j):
            ag_arrive(h, j, 6)
            ag_hop(h, j, 4)
            ag_arrive(h, j, 5)
            ag_hop(h, j, 1)
            ag_hop(h, j, 2)

    def ag_forward_last(h):
        @pl.loop(0, NF)
        def _(j):
            ag_arrive(h, j, 4)
            ag_hop(h, j, 0)

    def pack(h, first, last):
        if h == 0 and first == 0:
            for copy in raws:
                copy.wait()

        @pl.loop(first, last)
        def _(n):
            value = dot(p_own[0], raw[n])
            for o in range(8):
                act[h, n, o] = fold(value[o * rows : (o + 1) * rows, :]).astype(BF)

    def unfold_store(ref, h, j, k, pair):
        here = pl.ds(pl.multiple_of(h * cap + k * 2 * rows, 16), 2 * rows)
        mid = fw // 2
        for n in range(2):
            part = [v[n * rows : (n + 1) * rows, :] for v in pair]
            ref[j, here, n * mid : (n + 1) * mid] = jnp.concatenate(part, axis=0).astype(BF)

    def hidden(h):
        @pl.loop(0, 4 * NF)
        def _(i):
            j, k = i // 4, i % 4
            pair = []
            for n in range(2):
                g = act[h, 2 * j, 2 * k + n].astype(F32)
                u = act[h, 2 * j + 1, 2 * k + n].astype(F32)
                pair.append(g * jax.nn.sigmoid(g) * u)
            unfold_store(hid, h, j, k, pair)

    def gate_backward(h, j):
        @pl.loop(0, 4)
        def _(k):
            gates, ups = [], []
            for n in range(2):
                g = act[h, 2 * j, 2 * k + n].astype(F32)
                u = act[h, 2 * j + 1, 2 * k + n].astype(F32)
                d = dh[h, j, 2 * k + n].astype(F32)
                sig = jax.nn.sigmoid(g)
                gates.append(d * u * sig * (1.0 + g * (1.0 - sig)))
                ups.append(d * g * sig)
            unfold_store(dact, h, 2 * j, k, gates)
            unfold_store(dact, h, 2 * j + 1, k, ups)

    def half_copy(h, d):
        return remote(
            half_out.at[h, d], half_in.at[h, d], h_send.at[h, d], h_recv.at[h, d], at.sibling()
        )

    def unpack(h, d, core):
        value = term[h, d, :, :dw]
        high = value.astype(BF)
        low = (value - high.astype(F32)).astype(BF)
        back = p_back[pl.ds(pl.multiple_of(core * 256, 256), 256), :]
        return dot(back, high) + dot(back, low)

    def parts(h):
        here = half_rows(h)
        if h == 0:
            for copy in weights[1:]:
                copy.wait()

        @pl.loop(0, NF)
        def _(j):
            for e in (3, 1, 2, 0):
                ag_arrive(h, j, e)
            gate_backward(h, j)

            @pl.loop(0, ND)
            def _(d):
                units = pl.ds(pl.multiple_of(d * dw, dw), dw)
                value = dot_nt(dact[2 * j, here, :], wg[j, units, :])
                value = value + dot_nt(dact[2 * j + 1, here, :], wu[j, units, :])
                term[h, d, :, :dw] = value + jnp.where(j > 0, term[h, d, :, :dw], 0.0)

        @pl.loop(0, ND)
        def _(d):
            half_out[h, d] = unpack(h, d, 1 - at.core).astype(BF)
            half_copy(h, d).start()

    def mp_chunk(h, d, offset):
        owner = at.chip_at(-offset[0], offset[1])
        return term[h, d, pl.ds(pl.multiple_of(owner * 32, 32), 32), :dw]

    def mp_copy(h, d, e):
        src, dst = FLAT[e]
        return remote(
            mp_out.at[h, d, e],
            mp_in.at[h, d, e],
            m_send.at[h, d, e],
            m_recv.at[h, d, e],
            at.mp_hop(src, dst),
        )

    def mp_hop(h, d, e, value):
        mp_out[h, d, e] = value.astype(BF)
        mp_copy(h, d, e).start()

    def mp_arrive(h, d, e):
        arrival(mp_in.at[h, d, e], m_send.at[h, d, e], m_recv.at[h, d, e], at)
        return mp_in[h, d, e].astype(F32)

    def mp_leaves(h):
        @pl.loop(0, ND)
        def _(d):
            term[h, d, :256, :dw] = unpack(h, d, at.core)

        @pl.loop(0, ND)
        def _(d):
            half_copy(h, d).wait_recv()
            term[h, d, :256, :dw] = term[h, d, :256, :dw] + half_in[h, d].astype(F32)
            for e in (0, 1, 2, 6, 3):
                mp_hop(h, d, e, mp_chunk(h, d, FLAT[e][0]))

    def mp4(h):
        @pl.loop(0, ND)
        def _(d):
            mp_hop(h, d, 4, mp_chunk(h, d, (2, 0)) + mp_arrive(h, d, 0))

    def mp5(h):
        @pl.loop(0, ND)
        def _(d):
            mp_hop(h, d, 5, mp_chunk(h, d, (0, 1)) + mp_arrive(h, d, 1) + mp_arrive(h, d, 2))

    def mp_own(h):
        sums = []
        for d in range(ND):
            value = mp_chunk(h, d, (0, 0)) + mp_arrive(h, d, 3) + mp_arrive(h, d, 6)
            sums.append(value + mp_arrive(h, d, 4) + mp_arrive(h, d, 5))
        for k in range(4):
            both = jnp.concatenate([s[k * 8 : k * 8 + 8, :] for s in sums], axis=0)
            fin_out[2 * k + ((at.core + h) & 1)] = both.astype(BF)

    def tn(a, b):
        return lax.dot_general(a, b, (((0,), (0,)), ((), ())), preferred_element_type=F32).astype(BF)

    def out_copies(j):
        return [
            pltpu.make_async_copy(raw.at[2 * j], gg_out.at[:, piece(j)], out_sem.at[3 * j]),
            pltpu.make_async_copy(raw.at[2 * j + 1], gu_out.at[:, piece(j)], out_sem.at[3 * j + 1]),
            pltpu.make_async_copy(wd.at[piece(j), :], gd_out.at[piece(j), :], out_sem.at[3 * j + 2]),
        ]

    def weight_grad(j):
        for n in range(2):
            raw[2 * j + n] = tn(dyc[...], dact[2 * j + n])
            out_copies(j)[n].start()

    def down_grads():
        @pl.loop(0, NF)
        def _(j):
            wd[piece(j), :] = tn(hid[j], dyc[...])
            out_copies(j)[2].start()

    a, b = 0, 1
    one_hot(p_slab, a, a, True)
    one_hot(p_own, 0, a, False)
    gather_dy[a].stage(1)
    gather_dy[b].stage(1)
    for copy in weights[1:]:
        copy.start()
    pack(a, 0, NF)
    gather_dy[a].stage(2)
    gather_dy[b].stage(2)
    pack(a, NF, 2 * NF)
    gather_dy[a].stage(3)
    one_hot(p_slab, b, b, True)
    gather_dy[b].stage(3)
    one_hot(p_own, 0, b, False)
    gather_dy[a].stage(4)
    terms(a)
    gather_dy[b].stage(4)
    terms(b)
    for h in range(2):
        gather_x[h].stage(0)
    rs4(a)
    pack(b, 0, NF)
    rs5(a)
    rs6(a)
    rs4(b)
    for h in range(2):
        gather_x[h].stage(1)
    pack(b, NF, 2 * NF)
    rs5(b)
    rs_own(a)
    rs6(b)
    hidden(a)
    ag_forward(a)
    for h in range(2):
        gather_x[h].stage(2)
    hidden(b)
    rs_own(b)
    ag_forward_last(a)
    back_matrix(a)
    for h in range(2):
        gather_x[h].stage(3)
    ag_forward(b)
    parts(a)
    ag_forward_last(b)
    mp_leaves(a)
    back_matrix(b)
    down_grads()
    for h in range(2):
        gather_x[h].stage(4)
        dyc[half_rows(h), :] = dot(p_slab[h], xb[h]).astype(BF)
    mp4(a)
    parts(b)
    mp5(a)
    mp_leaves(b)
    mp_own(a)
    mp4(b)
    mp5(b)

    @pl.loop(0, NF)
    def _(j):
        weight_grad(j)

    mp_own(b)
    for k in (4, 3, 5, 2, 6, 1, 7):
        peer = lax.rem(at.dp + k, 8)
        sent.append(
            send(fin_out.at[peer], fin_in.at[at.dp], f_send.at[k], f_recv.at[k], {"dp": peer})
        )
    fin_in[at.dp] = fin_out[at.dp]
    for k in (4, 3, 5, 2, 6, 1, 7):
        source = lax.rem(at.dp + 8 - k, 8)
        arrival(fin_in.at[source], f_send.at[k], f_recv.at[k], at)
    for c in range(8):
        both = fin_in[c].astype(F32)
        for d in range(ND):
            gt_out[:, c * dl + d * dw : c * dl + (d + 1) * dw] = both[d * 8 : d * 8 + 8, :].astype(BF)
    for gather in gather_dy + gather_x:
        gather.drain()
    for copy in sent:
        copy.wait_send()

    @pl.loop(0, 2 * NF)
    def _(i):
        h, j = i // NF, i % NF
        for e in range(7):
            rs_copy(h, j, e).wait_send()
            ag_copy(h, j, e).wait_send()

    @pl.loop(0, 2 * ND)
    def _(i):
        h, d = i // ND, i % ND
        half_copy(h, d).wait_send()
        for e in range(7):
            mp_copy(h, d, e).wait_send()

    for j in range(NF):
        for copy in out_copies(j):
            copy.wait()


def main_call(size, number, tokens, out_grad, gate_pre, up_pre, wg, wu, wd, lengths):
    dl, fl = tokens.shape[1] // 8, gate_pre.shape[1]
    fw, dw, cap, rows = fl // NF, dl // ND, size // 2, size // 16
    dma = pltpu.SemaphoreType.DMA
    vmem, smem = pl.BlockSpec(memory_space=pltpu.VMEM), pl.BlockSpec(memory_space=pltpu.SMEM)
    anywhere = pl.BlockSpec(memory_space=pl.ANY)
    buffers = [
        (tokens.shape, BF),
        (tokens.shape, BF),
        ((8, 16, dl + 128), BF),
        ((8, 16, dl + 128), BF),
        ((2, 512, dl), BF),
        ((2, 512, dl), BF),
        ((2, cap, 512), BF),
        ((1, cap, 1024), BF),
        ((512, cap), BF),
        ((size, dl), BF),
        ((NF, dl, fw), BF),
        ((NF, dl, fw), BF),
        ((fl, dl), BF),
        ((2 * NF, 1024, fw), BF),
        ((2, 2 * NF, 8, 2 * rows, fw // 2), BF),
        ((NF, size, fw), BF),
        ((2 * NF, size, fw), BF),
        ((2, NF, cap, fw), F32),
        ((2, NF, 7, 2 * rows, fw // 2), BF),
        ((2, NF, 7, 2 * rows, fw // 2), BF),
        ((2, NF, 8, 2 * rows, fw // 2), BF),
        ((2, ND, 256, dw), BF),
        ((2, ND, 256, dw), BF),
        ((2, ND, 7, 32, dw), BF),
        ((2, ND, 7, 32, dw), BF),
        ((8, 16, dw), BF),
        ((8, 16, dw), BF),
    ]
    sems = [(2,), (8,), (8,), (1 + 2 * NF,), (2 * NF,), (3 * NF,)]
    sems += [(2, NF, 7)] * 4
    sems += [(2, 7), (2, 7), (2, 8), (2, 8)] * 2
    sems += [(2, ND), (2, ND), (2, ND, 7), (2, ND, 7), (8,), (8,)]
    return pl.pallas_call(
        main_kernel,
        out_shape=(
            jax.ShapeDtypeStruct((8, dl * 8), BF),
            jax.ShapeDtypeStruct((dl, fl), BF),
            jax.ShapeDtypeStruct((dl, fl), BF),
            jax.ShapeDtypeStruct((fl, dl), BF),
            jax.ShapeDtypeStruct((1,), jnp.int32),
        ),
        in_specs=[anywhere, anywhere, smem] + [anywhere] * 5,
        out_specs=(vmem,) + (anywhere,) * 3 + (smem,),
        scratch_shapes=[pltpu.VMEM(s, t) for s, t in buffers] + [dma(s) for s in sems],
        compiler_params=pltpu.CompilerParams(
            collective_id=number, has_side_effects=True, vmem_limit_bytes=63 * MIB
        ),
    )(tokens, out_grad, lengths, gate_pre, up_pre, wg, wu, wd)


def copy_kernel(*refs):
    count = len(refs) // 3
    bufs, (in_sem, out_sem) = refs[2 * count : 3 * count], refs[3 * count :]
    pieces = in_sem.shape[1]
    todo = []
    for n in range(count):
        src, dst, buf = refs[n], refs[count + n], bufs[n]
        rows = src.shape[0] // pieces
        for k in range(pieces):
            here = pl.ds(k * rows, rows)
            first = pltpu.make_async_copy(src.at[here, :], buf.at[here, :], in_sem.at[n, k])
            then = pltpu.make_async_copy(buf.at[here, :], dst.at[here, :], out_sem.at[n, k])
            first.start()
            todo.append((first, then))
    for first, then in todo:
        first.wait()
        then.start()
    for _, then in todo:
        then.wait()


def copy_out(arrays):
    anywhere = pl.BlockSpec(memory_space=pl.ANY)
    sem = pltpu.SemaphoreType.DMA((len(arrays), 4))
    return pl.pallas_call(
        copy_kernel,
        out_shape=tuple(jax.ShapeDtypeStruct(a.shape, a.dtype) for a in arrays),
        in_specs=[anywhere] * len(arrays),
        out_specs=(anywhere,) * len(arrays),
        scratch_shapes=[pltpu.VMEM(a.shape, a.dtype) for a in arrays] + [sem, sem],
        compiler_params=pltpu.CompilerParams(vmem_limit_bytes=60 * MIB),
    )(*arrays)


def local(*args):
    *outs, over = main_call(SIZE, 0, *args)

    def again(state):
        *full, _ = main_call(1024, 1, *args)
        return (jnp.int32(0), *full)

    _, grad_tokens, *grads = lax.while_loop(lambda state: state[0] > 0, again, (over[0], *outs))
    return (grad_tokens, *copy_out(grads))


def solution(mesh):
    in_specs = (
        P(("dp", "mp"), None),
        P(("dp", "mp"), None),
        P(None, "mp"),
        P(None, "mp"),
        P("dp", "mp"),
        P("dp", "mp"),
        P("mp", "dp"),
        P("dp"),
    )
    out_specs = (P(("dp", "mp"), None), P("dp", "mp"), P("dp", "mp"), P("mp", "dp"))
    return jax.shard_map(local, mesh=mesh, in_specs=in_specs, out_specs=out_specs, check_vma=False)
```

time: 532 us -> 102 us (0.19)
  waiting for transfers between devices: 326 us -> 0 us
  blocking collectives: 121 us -> 0 us
  Pallas kernels: 0 us -> 99.1 us
  matrix products: 33.9 us -> 0 us
  local copies, waits for them, and re-layouts: 26.4 us -> 0.67 us
  between operations: 14.7 us -> 1.35 us
  other arithmetic: 8.96 us -> 0 us
    psum x1 -> x0, waiting for transfers between devices: 258 us -> none  [local(): dh = lax.psum(term, 'dp')]
    all_to_all x3 -> x0, blocking collectives: 121 us -> none  [the longest x1 59.8 us: local(): lax.all_to_all(part_gate + part_up, 'dp', split_axis=0, concat_axis=1, ti...]
    pallas_call x0 -> x2, Pallas kernels: none -> 99.1 us  [the longest x1 91.8 us: main_call(): pl.pallas_call(main_kernel, out_shape=(jax.ShapeDtypeStruct((8, dl * 8),...]
    all_gather x2 -> x0, waiting for transfers between devices: 52 us -> none  [the longest x1 52 us: local(): lax.all_gather(masked, 'mp', axis=0, tiled=True)]
    dot_general x6 -> x0, matrix products: 33.9 us -> none  [the longest x1 8.42 us: local(): jnp.einsum('tf,td->fd', hidden, dy_cols, preferred_element_type=jnp.float32)]
    reduce_scatter x1 -> x0, waiting for transfers between devices: 15.1 us -> none  [local(): lax.psum_scatter(moved, 'mp', scatter_dimension=0, tiled=True)]
    all_to_all x3 -> x0, local copies, waits for them, and re-layouts: 10.8 us -> none  [the longest x1 4.61 us: local(): lax.all_to_all(block_x, 'dp', split_axis=1, concat_axis=0, tiled=True)]
    unnamed x22 -> x7, local copies, waits for them, and re-layouts: 8.29 us -> 0.67 us
  transfers between devices with their start and end apart: 4 -> 0, of which waited for: 3 -> 0; matrix products, arithmetic and copies ran while one was open for 9% -> 0% of each run, Pallas kernels for 0% -> 0%
where the time goes in v1:
time: 102 us
  Pallas kernels  99.1 us (97%)
  between operations  1.35 us (1%)
    pallas_call x1, Pallas kernels, main_call(): pl.pallas_call(main_kernel, out_shape=(jax.ShapeDtypeStruct((8, dl * 8),...  91.8 us
    pallas_call x1, Pallas kernels, copy_out(): pl.pallas_call(copy_kernel, out_shape=tuple((jax.ShapeDtypeStruct(a.shape...  7.33 us

profile of v1, /device:TPU:0, one launch (start us, length us, event | category | flops | bytes accessed | tf_op | source)
XLA Modules:
  0.0 102.0 jit_solution(13034822255911885057)
XLA Ops:
  1.3 0.0 copy-start
  1.3 0.0 copy-start.1
  1.3 91.8 %shard_map.111 = (bf16[8,8192]{1,0:T(8,128)(2,1)}, bf16[1024,1536]{1,0:T(8,128)(2,1)}, bf16[1024,1536]{1,0:T(8,128)(2,1)}, bf16[1536,1024]{1,0:T(8,128)(2,1)}, s32[1]{0:T(128)}) custom-call(bf16[8,8192]{1,0:T(8,128)(2,1)} %tok_hbm.1, bf16[8,8192]{1,0:T(8,128)(2,1)} %grad_hbm.1, s32[1]{0:T(128)S(6)} %copy.29.length, bf16[1024,1536]{1,0:T(8,128)(2,1)} %gp.1, ...), custom_call_target="tpu_custom_call" | custom-call | tf_op jit(solution)/shard_map/pallas_call | solution.py:734
  93.1 0.0 copy-done
  93.1 0.0 copy-done.1
  93.1 0.9 while.15
  94.0 0.0 copy-start.2
  94.0 7.3 %shard_map.112 = (bf16[1024,1536]{1,0:T(8,128)(2,1)}, bf16[1024,1536]{1,0:T(8,128)(2,1)}, bf16[1536,1024]{1,0:T(8,128)(2,1)}) custom-call(bf16[1024,1536]{1,0:T(8,128)(2,1)} %get-tuple-element.87.refs_0_, bf16[1024,1536]{1,0:T(8,128)(2,1)} %get-tuple-element.88.refs_1_, bf16[1536,1024]{1,0:T(8,128)(2,1)} %get-tuple-element.89.refs_2_), custom_call_target="tpu_custom_call" | custom-call | tf_op jit(solution)/shard_map/pallas_call | solution.py:776
  101.3 0.0 copy-done.2
  101.3 0.7 copy.31
Async XLA Ops:
  1.3 91.8 %copy-start = (bf16[8,8192]{1,0:T(8,128)(2,1)S(1)}, bf16[8,8192]{1,0:T(8,128)(2,1)}, u32[]{:S(2)}) copy-start(bf16[8,8192]{1,0:T(8,128)(2,1)} %tok_hbm.1) | copy-start | bytes 393220
  1.3 91.8 %copy-start.1 = (bf16[8,8192]{1,0:T(8,128)(2,1)S(1)}, bf16[8,8192]{1,0:T(8,128)(2,1)}, u32[]{:S(2)}) copy-start(bf16[8,8192]{1,0:T(8,128)(2,1)} %grad_hbm.1) | copy-start | bytes 393220
  94.0 7.3 %copy-start.2 = (bf16[8,8192]{1,0:T(8,128)(2,1)S(1)}, bf16[8,8192]{1,0:T(8,128)(2,1)}, u32[]{:S(2)}) copy-start(bf16[8,8192]{1,0:T(8,128)(2,1)} %get-tuple-element.175) | copy-start | bytes 393220

commit v2 on v1

v2 whole, which is shorter than its diff:
```python
import functools

import jax
import jax.numpy as jnp
from jax import lax
from jax.experimental import pallas as pl
from jax.experimental.pallas import tpu as pltpu
from jax.sharding import PartitionSpec as P

SEQ_LEN = 128
NZ, NY = 4, 2
NF = 2
ND = 2
SIZE = 640
BF, F32 = jnp.bfloat16, jnp.float32
MIB = 1 << 20

class Tree:
    def __init__(self, hops=()):
        nodes = [(a, b) for b in (1, 0) for a in (2, 1, 3, 0)][:-1]
        to = {node: (0, 0) for node in nodes}
        to.update(hops)
        self.to, self.nodes = to, sorted(nodes, key=lambda node: (-self.depth(node, to), node[0] != 2))
        self.leaves = [n for n in self.nodes if not self.children(n)]
        self.inner = [n for n in self.nodes if self.children(n)]
        self.levels = max(self.depth(n, to) for n in nodes)

    def depth(self, node, to=None):
        to = to or self.to
        return 0 if node == (0, 0) else 1 + self.depth(to[node], to)

    def children(self, node):
        return [n for n in self.nodes if self.to[n] == node]

    def index(self, node):
        return self.nodes.index(node)


DEEP = Tree(
    hops=(((2, 1), (2, 0)), ((1, 1), (0, 1)), ((3, 1), (0, 1)), ((2, 0), (1, 0)))
)
FLAT = Tree(hops=(((2, 1), (2, 0)), ((1, 1), (0, 1)), ((3, 1), (0, 1))))
ROWS = Tree(hops=(((2, 1), (0, 1)), ((1, 1), (0, 1)), ((3, 1), (0, 1))))
STAR = Tree()
REDUCE = (FLAT, DEEP)
SPREAD = (DEEP, FLAT)
DY_TREE = (FLAT, FLAT)
X_TREE = (ROWS, ROWS)
HOME = (ROWS, FLAT)


class Place:
    def __init__(self):
        self.dp = lax.axis_index("dp")
        self.mp = lax.axis_index("mp")
        self.z, self.yl = self.dp // NY, self.dp % NY
        self.core = self.mp % 2
        self.chip = self.mp // 2
        self.yh, self.x = self.chip // 4, self.chip % 4
        self.sign = 1 - 2 * self.core

    def dp_at(self, da, db):
        z = lax.rem(self.z + self.sign * da + 4, 4)
        return z * NY + (1 - self.yl if db else self.yl)

    def chip_at(self, da, db):
        x = lax.rem(self.x + self.sign * da + 4, 4)
        return (1 - self.yh if db else self.yh) * 4 + x

    def dp_hop(self, src, dst):
        return {"dp": self.dp_at(dst[0] - src[0], src[1] ^ dst[1])}

    def mp_hop(self, src, dst):
        return {"mp": self.chip_at(dst[0] - src[0], src[1] ^ dst[1]) * 2 + self.core}

    def sibling(self):
        return {"mp": self.chip * 2 + 1 - self.core}

    def greet(self):
        sem = pltpu.get_barrier_semaphore()
        peers = [{"dp": lax.rem(self.dp + k, 8)} for k in range(1, 8)]
        peers += [self.sibling()]
        peers += [{"mp": self.chip_at(a, b) * 2 + self.core} for a, b in STAR.nodes]
        for peer in peers:
            pl.semaphore_signal(sem, inc=1, device_id=peer, device_id_type=pl.DeviceIdType.MESH)
        self.peers = len(peers)

    def meet(self):
        pl.semaphore_wait(pltpu.get_barrier_semaphore(), self.peers)


def remote(src, dst, send_sem, recv_sem, device):
    return pltpu.make_async_remote_copy(
        src_ref=src,
        dst_ref=dst,
        send_sem=send_sem,
        recv_sem=recv_sem,
        device_id=device,
        device_id_type=pl.DeviceIdType.MESH,
    )


def send(*args):
    copy = remote(*args)
    copy.start()
    return copy


def dot_nt(a, b):
    return lax.dot_general(a, b, (((1,), (1,)), ((), ())), preferred_element_type=F32)


def dot(a, b):
    return jnp.dot(a, b, preferred_element_type=F32)


class Gather:
    def __init__(self, at, tree, buf, rows, sems):
        self.at, self.tree, self.buf, self.rows = at, tree, buf, rows
        self.send_sem, self.recv_sem, self.sib_send, self.sib_recv = sems
        self.copies = []

    def slab(self, chip, core):
        start = pl.multiple_of((core * 8 + chip) * self.rows, self.rows)
        return self.buf.at[pl.ds(start, self.rows), :]

    def slab_from(self, node):
        return self.slab(self.at.chip_at(-node[0], node[1]), self.at.core)

    def pass_on(self, node):
        ref = self.slab_from(node)
        for child in self.tree.children(node):
            n = self.tree.index(child)
            to = self.at.mp_hop(node, child)
            self.copies.append(send(ref, ref, self.send_sem.at[n], self.recv_sem.at[n], to))
        n = 7 if node == (0, 0) else self.tree.index(node)
        self.copies.append(
            send(ref, ref, self.sib_send.at[n], self.sib_recv.at[n], self.at.sibling())
        )

    def start(self, value):
        start = pl.multiple_of((self.at.core * 8 + self.at.chip) * self.rows, self.rows)
        self.buf[pl.ds(start, self.rows), :] = value
        self.pass_on((0, 0))

    def relay(self, level):
        for node in self.tree.nodes:
            if self.tree.depth(node) == level:
                n = self.tree.index(node)
                arrival(self.slab_from(node), self.send_sem.at[n], self.recv_sem.at[n], self.at)
                self.pass_on(node)

    def finish(self):
        for n, (a, b) in enumerate(self.tree.nodes + [(0, 0)]):
            ref = self.slab(self.at.chip_at(a, b), 1 - self.at.core)
            arrival(ref, self.sib_send.at[n], self.sib_recv.at[n], self.at)

    def drain(self):
        for copy in self.copies:
            copy.wait_send()


def arrival(ref, send_sem, recv_sem, at):
    remote(ref, ref, send_sem, recv_sem, at.sibling()).wait_recv()


def live_rows(length, parity):
    rest = length & 15
    extra = jnp.where(parity == 0, jnp.minimum(rest, 8), jnp.maximum(rest - 8, 0))
    return (length >> 4) * 8 + extra


def rank_of(index, lens, h, slabs):
    if slabs:
        slab = index >> 5
        core = slab >> 3
        response = ((index >> 3) & 3) * 2 + ((core + h) & 1)
        place = ((slab & 7) * 2 + core) * 8 + (index & 7)
    else:
        response = index >> 7
        place = index & 127
    rank = jnp.full(index.shape, -1, jnp.int32)
    first = 0
    for r in range(8):
        parity = (r + h) & 1
        live = (response == r) & (place < lens[r]) & (((place >> 3) & 1) == parity)
        rank = jnp.where(live, (place >> 4) * 8 + (place & 7) + first, rank)
        first = first + live_rows(lens[r], parity)
    return rank


def fold(value):
    mid = value.shape[1] // 2
    return jnp.concatenate([value[:, :mid], value[:, mid:]], axis=0)


def main_kernel(
    tok_hbm,
    grad_hbm,
    length,
    gp,
    up,
    wg_hbm,
    wu_hbm,
    wd_hbm,
    gt_out,
    gg_out,
    gu_out,
    gd_out,
    over_out,
    tok,
    grad,
    sbuf,
    rbuf,
    sbuf_x,
    rbuf_x,
    dyb,
    xb,
    p_slab,
    p_own,
    p_back,
    dyc,
    wg,
    wu,
    act,
    hid,
    dact,
    term,
    rs_out,
    rs_in,
    dh,
    half_out,
    half_in,
    mp_out,
    mp_in,
    fin_out,
    fin_in,
    in_sem,
    a_send,
    a_recv,
    ax_send,
    ax_recv,
    w_sem,
    raw_sem,
    rs_send,
    rs_recv,
    ag_send,
    ag_recv,
    dy_send,
    dy_recv,
    dys_send,
    dys_recv,
    x_send,
    x_recv,
    xs_send,
    xs_recv,
    h_send,
    h_recv,
    m_send,
    m_recv,
    f_send,
    f_recv,
):
    at = Place()
    cap = dyc.shape[0] // 2
    rows = cap // 8
    fw = term.shape[3]
    dl = dyc.shape[1]
    dw = dl // ND
    sent = []

    loads = [
        pltpu.make_async_copy(src, dst, in_sem.at[n])
        for n, (src, dst) in enumerate(((tok_hbm, tok), (grad_hbm, grad)))
    ]
    for copy in loads:
        copy.start()
    at.greet()
    own_len = jnp.full((16, 128), length[0], jnp.int32).astype(F32).astype(BF)
    loads[1].wait()
    for c in range(8):
        sbuf[c, :, :dw] = fold(grad[:, c * dl : (c + 1) * dl].astype(F32)).astype(BF)
        sbuf[c, :, dw:] = own_len
    at.meet()

    def to_dp(src, dst, send_sem, recv_sem):
        for k in (4, 3, 5, 2, 6, 1, 7):
            peer = lax.rem(at.dp + k, 8)
            sent.append(
                send(src.at[peer], dst.at[at.dp], send_sem.at[k], recv_sem.at[k], {"dp": peer})
            )
        dst[at.dp] = src[at.dp]

    def from_dp(dst, send_sem, recv_sem):
        for k in (4, 3, 5, 2, 6, 1, 7):
            source = lax.rem(at.dp + 8 - k, 8)
            arrival(dst.at[source], send_sem.at[k], recv_sem.at[k], at)

    to_dp(sbuf, rbuf, a_send, a_recv)
    loads[0].wait()
    for c in range(8):
        sbuf_x[c] = fold(tok[:, c * dl : (c + 1) * dl].astype(F32)).astype(BF)

    def piece(j):
        return pl.ds(pl.multiple_of(j * fw, fw), fw)

    weights = [pltpu.make_async_copy(wd_hbm, gd_out, w_sem.at[0])]
    for j in range(NF):
        for n, (src, dst) in enumerate(((wg_hbm, wg), (wu_hbm, wu))):
            sem = w_sem.at[1 + 2 * j + n]
            weights.append(pltpu.make_async_copy(src.at[:, piece(j)], dst.at[j], sem))
    raws = [
        pltpu.make_async_copy(src, dst, raw_sem.at[n])
        for n, (src, dst) in enumerate(((gp, gg_out), (up, gu_out)))
    ]
    weights[0].start()
    for copy in raws:
        copy.start()
    from_dp(rbuf, a_send, a_recv)

    def slab_of(buf, h):
        parity = (at.core + h) & 1
        blocks = []
        for k in range(4):
            value = buf[2 * k + parity].astype(F32)
            blocks.append(jnp.concatenate([value[:8, :dw], value[8:, :dw]], axis=1))
        return jnp.concatenate(blocks, axis=0).astype(BF)

    def one_hot(ref, slot, h, slabs):
        size = ref.shape[2]
        rank = rank_of(lax.broadcasted_iota(jnp.int32, (1, size), 1), lens, h, slabs)
        blk = 64

        @pl.loop(0, cap // blk)
        def _(i):
            start = pl.multiple_of(i * blk, blk)
            index = lax.broadcasted_iota(jnp.int32, (blk, size), 0) + start
            ref[slot, pl.ds(start, blk), :] = jnp.where(index == rank, 1.0, 0.0).astype(BF)

    def back_matrix(h):
        blk = 128

        @pl.loop(0, 512 // blk)
        def _(i):
            start = pl.multiple_of(i * blk, blk)
            index = lax.broadcasted_iota(jnp.int32, (blk, 1), 0) + start
            rank = rank_of(index, lens, h, True)
            lane = lax.broadcasted_iota(jnp.int32, (blk, cap), 1)
            p_back[pl.ds(start, blk), :] = jnp.where(lane == rank, 1.0, 0.0).astype(BF)

    gather_dy, gather_x = [], []
    for h in range(2):
        sems = [sem.at[h] for sem in (dy_send, dy_recv, dys_send, dys_recv)]
        gather_dy.append(Gather(at, DY_TREE[h], dyb.at[h], 32, sems))
        sems = [sem.at[h] for sem in (x_send, x_recv, xs_send, xs_recv)]
        gather_x.append(Gather(at, X_TREE[h], xb.at[h], 32, sems))
    gather_dy[0].start(slab_of(rbuf, 0))
    to_dp(sbuf_x, rbuf_x, ax_send, ax_recv)
    lens = [jnp.max(rbuf[r].astype(F32)[0:1, dw:]).astype(jnp.int32) for r in range(8)]
    need = [sum(live_rows(lens[r], (r + h) & 1) for r in range(8)) for h in range(2)]
    over_out[0] = (jnp.maximum(need[0], need[1]) > cap).astype(jnp.int32)

    def half_rows(h):
        return slice(h * cap, (h + 1) * cap)

    def chunk(h, j, offset):
        owner = at.dp_at(-offset[0], offset[1])
        return fold(term[h, j, pl.ds(pl.multiple_of(owner * rows, rows), rows), :])

    def rs_copy(h, j, node):
        e = REDUCE[h].index(node)
        return remote(
            rs_out.at[h, j, e],
            rs_in.at[h, j, e],
            rs_send.at[h, j, e],
            rs_recv.at[h, j, e],
            at.dp_hop(node, REDUCE[h].to[node]),
        )

    def rs_sum(h, j, node):
        value = chunk(h, j, node)
        for child in REDUCE[h].children(node):
            e = REDUCE[h].index(child)
            arrival(rs_in.at[h, j, e], rs_send.at[h, j, e], rs_recv.at[h, j, e], at)
            value = value + rs_in[h, j, e].astype(F32)
        return value

    def rs_hop(h, j, node):
        rs_out[h, j, REDUCE[h].index(node)] = rs_sum(h, j, node).astype(BF)
        rs_copy(h, j, node).start()

    def terms(h):
        dyc[half_rows(h), :] = dot(p_slab[h], dyb[h]).astype(BF)
        if h == 0:
            weights[0].wait()

        @pl.loop(0, NF)
        def _(j):
            term[h, j] = dot_nt(dyc[half_rows(h), :], gd_out[piece(j), :])
            for node in REDUCE[h].leaves:
                rs_hop(h, j, node)

    def rs_inner(h, n):
        @pl.loop(0, NF)
        def _(j):
            for node in REDUCE[h].inner[n : n + 1]:
                rs_hop(h, j, node)

    def ag_ref(h, j, offset):
        return dh.at[h, j, at.dp_at(-offset[0], offset[1])]

    def ag_copy(h, j, node):
        e = SPREAD[h].index(node)
        ref = ag_ref(h, j, SPREAD[h].to[node])
        to = at.dp_hop(SPREAD[h].to[node], node)
        return remote(ref, ref, ag_send.at[h, j, e], ag_recv.at[h, j, e], to)

    def ag_arrive(h, j, node):
        e = SPREAD[h].index(node)
        arrival(ag_ref(h, j, node), ag_send.at[h, j, e], ag_recv.at[h, j, e], at)

    def ag_pass_on(h, j, node):
        for child in SPREAD[h].children(node):
            ag_copy(h, j, child).start()

    def rs_own(h):
        @pl.loop(0, NF)
        def _(j):
            dh[h, j, at.dp] = rs_sum(h, j, (0, 0)).astype(BF)
            ag_pass_on(h, j, (0, 0))

    def ag_forward(h, level):
        @pl.loop(0, NF)
        def _(j):
            for node in SPREAD[h].inner:
                if SPREAD[h].depth(node) == level:
                    ag_arrive(h, j, node)
                    ag_pass_on(h, j, node)

    def pack(h, which):
        if h == 0:
            raws[which].wait()

        @pl.loop(0, NF)
        def _(j):
            value = dot(p_own[0], (gg_out, gu_out)[which][:, piece(j)])
            for o in range(8):
                act[h, 2 * j + which, o] = fold(value[o * rows : (o + 1) * rows, :]).astype(BF)

    def unfold_store(ref, h, j, k, pair):
        here = pl.ds(pl.multiple_of(h * cap + k * 2 * rows, 16), 2 * rows)
        mid = fw // 2
        for n in range(2):
            part = [v[n * rows : (n + 1) * rows, :] for v in pair]
            ref[j, here, n * mid : (n + 1) * mid] = jnp.concatenate(part, axis=0).astype(BF)

    def hidden(h):
        @pl.loop(0, 4 * NF)
        def _(i):
            j, k = i // 4, i % 4
            pair = []
            for n in range(2):
                g = act[h, 2 * j, 2 * k + n].astype(F32)
                u = act[h, 2 * j + 1, 2 * k + n].astype(F32)
                pair.append(g * jax.nn.sigmoid(g) * u)
            unfold_store(hid, h, j, k, pair)

    def gate_backward(h, j):
        @pl.loop(0, 4)
        def _(k):
            gates, ups = [], []
            for n in range(2):
                g = act[h, 2 * j, 2 * k + n].astype(F32)
                u = act[h, 2 * j + 1, 2 * k + n].astype(F32)
                d = dh[h, j, 2 * k + n].astype(F32)
                sig = jax.nn.sigmoid(g)
                gates.append(d * u * sig * (1.0 + g * (1.0 - sig)))
                ups.append(d * g * sig)
            unfold_store(dact, h, 2 * j, k, gates)
            unfold_store(dact, h, 2 * j + 1, k, ups)

    def half_copy(h, d):
        return remote(
            half_out.at[h, d], half_in.at[h, d], h_send.at[h, d], h_recv.at[h, d], at.sibling()
        )

    def unpack(h, d, core):
        value = term[h, d, :, :dw]
        high = value.astype(BF)
        low = (value - high.astype(F32)).astype(BF)
        back = p_back[pl.ds(pl.multiple_of(core * 256, 256), 256), :]
        return dot(back, high) + dot(back, low)

    def parts(h):
        here = half_rows(h)
        if h == 0:
            for copy in weights[1:]:
                copy.wait()

        def arrived(j):
            for node in reversed(SPREAD[h].leaves):
                ag_arrive(h, j, node)
            gate_backward(h, j)

        def part(j, d):
            units = pl.ds(pl.multiple_of(d * dw, dw), dw)
            value = dot_nt(dact[2 * j, here, :], wg[j, units, :])
            return value + dot_nt(dact[2 * j + 1, here, :], wu[j, units, :])

        for j in range(NF - 1):
            arrived(j)

            @pl.loop(0, ND)
            def _(d):
                value = part(j, d)
                term[h, d, :, :dw] = value + term[h, d, :, :dw] if j else value

        arrived(NF - 1)

        @pl.loop(0, ND)
        def _(d):
            term[h, d, :, :dw] = term[h, d, :, :dw] + part(NF - 1, d)
            half_out[h, d] = unpack(h, d, 1 - at.core).astype(BF)
            half_copy(h, d).start()

    def mp_chunk(h, d, offset):
        owner = at.chip_at(-offset[0], offset[1])
        return term[h, d, pl.ds(pl.multiple_of(owner * 32, 32), 32), :dw]

    def mp_copy(h, d, node):
        e = HOME[h].index(node)
        return remote(
            mp_out.at[h, d, e],
            mp_in.at[h, d, e],
            m_send.at[h, d, e],
            m_recv.at[h, d, e],
            at.mp_hop(node, HOME[h].to[node]),
        )

    def mp_sum(h, d, node):
        value = mp_chunk(h, d, node)
        for child in HOME[h].children(node):
            e = HOME[h].index(child)
            arrival(mp_in.at[h, d, e], m_send.at[h, d, e], m_recv.at[h, d, e], at)
            value = value + mp_in[h, d, e].astype(F32)
        return value

    def mp_hop(h, d, node):
        mp_out[h, d, HOME[h].index(node)] = mp_sum(h, d, node).astype(BF)
        mp_copy(h, d, node).start()

    def mp_leaves(h):
        @pl.loop(0, ND)
        def _(d):
            value = unpack(h, d, at.core)
            half_copy(h, d).wait_recv()
            term[h, d, :256, :dw] = value + half_in[h, d].astype(F32)
            for node in HOME[h].leaves:
                mp_hop(h, d, node)

    def mp_inner(h):
        if HOME[h].inner:

            @pl.loop(0, ND)
            def _(d):
                for node in HOME[h].inner:
                    mp_hop(h, d, node)

    def mp_own(h):
        sums = [mp_sum(h, d, (0, 0)) for d in range(ND)]
        for k in range(4):
            both = jnp.concatenate([s[k * 8 : k * 8 + 8, :] for s in sums], axis=0)
            fin_out[2 * k + ((at.core + h) & 1)] = both.astype(BF)

    def tn(a, b):
        return lax.dot_general(a, b, (((0,), (0,)), ((), ())), preferred_element_type=F32).astype(BF)

    def weight_grad(j):
        for n, out in enumerate((gg_out, gu_out)):
            out[:, piece(j)] = tn(dyc[...], dact[2 * j + n])

    def down_grads():
        @pl.loop(0, NF)
        def _(j):
            gd_out[piece(j), :] = tn(hid[j], dyc[...])

    a, b = 0, 1
    one_hot(p_slab, a, a, True)
    one_hot(p_own, 0, a, False)
    pack(a, 0)
    gather_dy[b].start(slab_of(rbuf, b))
    for copy in weights[1:]:
        copy.start()
    pack(a, 1)
    one_hot(p_slab, b, b, True)
    for level in range(1, DY_TREE[a].levels + 1):
        gather_dy[a].relay(level)
    gather_dy[b].relay(1)
    gather_dy[a].finish()
    terms(a)
    for level in range(2, DY_TREE[b].levels + 1):
        gather_dy[b].relay(level)
    one_hot(p_own, 0, b, False)
    rs_inner(a, 0)
    gather_dy[b].finish()
    rs_inner(a, 1)
    terms(b)
    rs_inner(a, 2)
    from_dp(rbuf_x, ax_send, ax_recv)
    for h in range(2):
        gather_x[h].start(slab_of(rbuf_x, h))
    pack(b, 0)
    rs_own(a)
    rs_inner(b, 0)
    rs_inner(b, 1)
    pack(b, 1)
    rs_inner(b, 2)
    hidden(a)
    ag_forward(a, 1)
    hidden(b)
    rs_own(b)
    ag_forward(a, 2)
    for h in range(2):
        gather_x[h].relay(1)
    down_grads()
    ag_forward(b, 1)
    back_matrix(a)
    parts(a)
    ag_forward(b, 2)
    for h in range(2):
        gather_x[h].relay(2)
    mp_leaves(a)
    back_matrix(b)
    for h in range(2):
        gather_x[h].finish()
        dyc[half_rows(h), :] = dot(p_slab[h], xb[h]).astype(BF)
    parts(b)
    mp_inner(a)
    mp_leaves(b)
    mp_own(a)

    def weight_grads(first, last):
        @pl.loop(first, last)
        def _(j):
            weight_grad(j)

    mp_inner(b)
    weight_grads(0, 1)
    mp_own(b)
    to_dp(fin_out, fin_in, f_send, f_recv)
    weight_grads(1, NF)
    for gather in gather_dy + gather_x:
        gather.drain()

    for h in range(2):

        @pl.loop(0, NF)
        def _(j):
            for node in STAR.nodes:
                rs_copy(h, j, node).wait_send()
                ag_copy(h, j, node).wait_send()

        @pl.loop(0, ND)
        def _(d):
            half_copy(h, d).wait_send()
            for node in STAR.nodes:
                mp_copy(h, d, node).wait_send()

    from_dp(fin_in, f_send, f_recv)
    for c in range(8):
        both = fin_in[c].astype(F32)
        for d in range(ND):
            gt_out[:, c * dl + d * dw : c * dl + (d + 1) * dw] = both[d * 8 : d * 8 + 8, :].astype(BF)
    for copy in sent:
        copy.wait_send()


def main_call(size, number, tokens, out_grad, gate_pre, up_pre, wg, wu, wd, lengths):
    dl, fl = tokens.shape[1] // 8, gate_pre.shape[1]
    fw, dw, cap, rows = fl // NF, dl // ND, size // 2, size // 16
    dma = pltpu.SemaphoreType.DMA
    vmem, smem = pl.BlockSpec(memory_space=pltpu.VMEM), pl.BlockSpec(memory_space=pltpu.SMEM)
    anywhere = pl.BlockSpec(memory_space=pl.ANY)
    buffers = [
        (tokens.shape, BF),
        (tokens.shape, BF),
        ((8, 16, dw + 128), BF),
        ((8, 16, dw + 128), BF),
        ((8, 16, dw), BF),
        ((8, 16, dw), BF),
        ((2, 512, dl), BF),
        ((2, 512, dl), BF),
        ((2, cap, 512), BF),
        ((1, cap, 1024), BF),
        ((512, cap), BF),
        ((size, dl), BF),
        ((NF, dl, fw), BF),
        ((NF, dl, fw), BF),
        ((2, 2 * NF, 8, 2 * rows, fw // 2), BF),
        ((NF, size, fw), BF),
        ((2 * NF, size, fw), BF),
        ((2, NF, cap, fw), F32),
        ((2, NF, 7, 2 * rows, fw // 2), BF),
        ((2, NF, 7, 2 * rows, fw // 2), BF),
        ((2, NF, 8, 2 * rows, fw // 2), BF),
        ((2, ND, 256, dw), BF),
        ((2, ND, 256, dw), BF),
        ((2, ND, 7, 32, dw), BF),
        ((2, ND, 7, 32, dw), BF),
        ((8, 16, dw), BF),
        ((8, 16, dw), BF),
    ]
    sems = [(2,), (8,), (8,), (8,), (8,), (1 + 2 * NF,), (2,)]
    sems += [(2, NF, 7)] * 4
    sems += [(2, 7), (2, 7), (2, 8), (2, 8)] * 2
    sems += [(2, ND), (2, ND), (2, ND, 7), (2, ND, 7), (8,), (8,)]
    return pl.pallas_call(
        main_kernel,
        out_shape=(
            jax.ShapeDtypeStruct((8, dl * 8), BF),
            jax.ShapeDtypeStruct((dl, fl), BF),
            jax.ShapeDtypeStruct((dl, fl), BF),
            jax.ShapeDtypeStruct((fl, dl), BF),
            jax.ShapeDtypeStruct((1,), jnp.int32),
        ),
        in_specs=[anywhere, anywhere, smem] + [anywhere] * 5,
        out_specs=(vmem,) * 4 + (smem,),
        scratch_shapes=[pltpu.VMEM(s, t) for s, t in buffers] + [dma(s) for s in sems],
        compiler_params=pltpu.CompilerParams(
            collective_id=number, has_side_effects=True, vmem_limit_bytes=(38 if size <= SIZE else 63) * MIB
        ),
    )(tokens, out_grad, lengths, gate_pre, up_pre, wg, wu, wd)


def copy_kernel(*refs):
    sem, refs = refs[-1], refs[:-1]
    count = len(refs) // 2
    copies = [
        pltpu.make_async_copy(refs[n], refs[count + n], sem.at[n]) for n in range(count)
    ]
    for copy in copies:
        copy.start()
    for copy in copies:
        copy.wait()


def copy_out(arrays):
    anywhere = pl.BlockSpec(memory_space=pl.ANY)
    return pl.pallas_call(
        copy_kernel,
        out_shape=tuple(jax.ShapeDtypeStruct(a.shape, a.dtype) for a in arrays),
        in_specs=[pl.BlockSpec(memory_space=pltpu.VMEM)] * len(arrays),
        out_specs=(anywhere,) * len(arrays),
        scratch_shapes=[pltpu.SemaphoreType.DMA((len(arrays),))],
        compiler_params=pltpu.CompilerParams(vmem_limit_bytes=24 * MIB),
    )(*arrays)


def local(*args):
    *outs, over = main_call(SIZE, 0, *args)

    def again(state):
        *full, _ = main_call(1024, 1, *args)
        return (jnp.int32(0), *copy_out(full))

    state = (over[0], *copy_out(outs))
    return lax.while_loop(lambda state: state[0] > 0, again, state)[1:]


def solution(mesh):
    in_specs = (
        P(("dp", "mp"), None),
        P(("dp", "mp"), None),
        P(None, "mp"),
        P(None, "mp"),
        P("dp", "mp"),
        P("dp", "mp"),
        P("mp", "dp"),
        P("dp"),
    )
    out_specs = (P(("dp", "mp"), None), P("dp", "mp"), P("dp", "mp"), P("mp", "dp"))
    return jax.shard_map(local, mesh=mesh, in_specs=in_specs, out_specs=out_specs, check_vma=False)
```

time: 102 us -> 89.5 us (0.88)
  Pallas kernels: 99.1 us -> 87.2 us
    pallas_call x1, Pallas kernels: 91.8 us -> 83.4 us  [main_call(): pl.pallas_call(main_kernel, out_shape=(jax.ShapeDtypeStruct((8, dl * 8),...]
    pallas_call x1, Pallas kernels: 7.33 us -> 3.82 us  [copy_out(): pl.pallas_call(copy_kernel, out_shape=tuple((jax.ShapeDtypeStruct(a.shape...]
where the time goes in v2:
time: 89.5 us; the launch traced here: 89.4 us
  Pallas kernels  87.2 us (97%)
  between operations  1.48 us (2%)
    pallas_call x1, Pallas kernels, main_call(): pl.pallas_call(main_kernel, out_shape=(jax.ShapeDtypeStruct((8, dl * 8),...  83.4 us
    pallas_call x1, Pallas kernels, copy_out(): pl.pallas_call(copy_kernel, out_shape=tuple((jax.ShapeDtypeStruct(a.shape...  3.82 us

profile of v2, /device:TPU:0, one launch (start us, length us, event | category | flops | bytes accessed | tf_op | source)
XLA Modules:
  0.0 89.4 jit_solution(17321153678495714494)
XLA Ops:
  1.3 83.4 %shard_map.111 = (bf16[8,8192]{1,0:T(8,128)(2,1)S(1)}, bf16[1024,1536]{1,0:T(8,128)(2,1)S(1)}, bf16[1024,1536]{1,0:T(8,128)(2,1)S(1)}, bf16[1536,1024]{1,0:T(8,128)(2,1)S(1)}, s32[1]{0:T(128)}) custom-call(bf16[8,8192]{1,0:T(8,128)(2,1)} %tok_hbm.1, bf16[8,8192]{1,0:T(8,128)(2,1)} %grad_hbm.1, s32[1]{0:T(128)S(6)} %copy.28.length, bf16[1024,1536]{1,0:T(8,128)(2,1)} %gp.1, ...), custom_call_target="tpu_custom_call" | custom-call | tf_op jit(solution)/shard_map/pallas_call | solution.py:717
  84.7 0.0 copy-start.4
  84.7 0.0 copy-start.5
  84.7 3.8 %shard_map.112 = (bf16[8,8192]{1,0:T(8,128)(2,1)}, bf16[1024,1536]{1,0:T(8,128)(2,1)}, bf16[1024,1536]{1,0:T(8,128)(2,1)}, bf16[1536,1024]{1,0:T(8,128)(2,1)}) custom-call(bf16[8,8192]{1,0:T(8,128)(2,1)S(1)} %get-tuple-element.87.refs_0_, bf16[1024,1536]{1,0:T(8,128)(2,1)S(1)} %get-tuple-element.88.refs_1_, ...), custom_call_target="tpu_custom_call" | custom-call | tf_op jit(solution)/shard_map/pallas_call | solution.py:749
  88.5 0.0 copy-done.4
  88.5 0.0 copy-done.5
  88.5 0.7 while.15
Async XLA Ops:
  84.7 3.8 %copy-start.4 = (bf16[8,8192]{1,0:T(8,128)(2,1)S(1)}, bf16[8,8192]{1,0:T(8,128)(2,1)}, u32[]{:S(2)}) copy-start(bf16[8,8192]{1,0:T(8,128)(2,1)} %tok_hbm.1) | copy-start | bytes 393220
  84.7 3.8 %copy-start.5 = (bf16[8,8192]{1,0:T(8,128)(2,1)S(1)}, bf16[8,8192]{1,0:T(8,128)(2,1)}, u32[]{:S(2)}) copy-start(bf16[8,8192]{1,0:T(8,128)(2,1)} %grad_hbm.1) | copy-start | bytes 393220

commit v3 on v2

--- a/solution.py
+++ b/solution.py
@@ -593,6 +593,7 @@
         copy.start()
     pack(a, 1)
     one_hot(p_slab, b, b, True)
+    back_matrix(a)
     for level in range(1, DY_TREE[a].levels + 1):
         gather_dy[a].relay(level)
     gather_dy[b].relay(1)
@@ -606,12 +607,12 @@
     rs_inner(a, 1)
     terms(b)
     rs_inner(a, 2)
+    pack(b, 0)
+    rs_own(a)
+    rs_inner(b, 0)
     from_dp(rbuf_x, ax_send, ax_recv)
     for h in range(2):
         gather_x[h].start(slab_of(rbuf_x, h))
-    pack(b, 0)
-    rs_own(a)
-    rs_inner(b, 0)
     rs_inner(b, 1)
     pack(b, 1)
     rs_inner(b, 2)
@@ -619,24 +620,23 @@
     ag_forward(a, 1)
     hidden(b)
     rs_own(b)
+    down_grads()
     ag_forward(a, 2)
     for h in range(2):
         gather_x[h].relay(1)
-    down_grads()
     ag_forward(b, 1)
-    back_matrix(a)
     parts(a)
     ag_forward(b, 2)
     for h in range(2):
         gather_x[h].relay(2)
     mp_leaves(a)
     back_matrix(b)
+    parts(b)
+    mp_inner(a)
+    mp_leaves(b)
     for h in range(2):
         gather_x[h].finish()
         dyc[half_rows(h), :] = dot(p_slab[h], xb[h]).astype(BF)
-    parts(b)
-    mp_inner(a)
-    mp_leaves(b)
     mp_own(a)
 
     def weight_grads(first, last):

time: 89.5 us -> 88.2 us (0.985)
  Pallas kernels: 87.2 us -> 85.9 us
    pallas_call x1, Pallas kernels: 83.4 us -> 82.1 us  [main_call(): pl.pallas_call(main_kernel, out_shape=(jax.ShapeDtypeStruct((8, dl * 8),...]
where the time goes in v3:
time: 88.2 us; the launch traced here: 88.1 us
  Pallas kernels  85.9 us (97%)
  between operations  1.48 us (2%)
    pallas_call x1, Pallas kernels, main_call(): pl.pallas_call(main_kernel, out_shape=(jax.ShapeDtypeStruct((8, dl * 8),...  82.1 us
    pallas_call x1, Pallas kernels, copy_out(): pl.pallas_call(copy_kernel, out_shape=tuple((jax.ShapeDtypeStruct(a.shape...  3.82 us

profile of v3, /device:TPU:0, one launch (start us, length us, event | category | flops | bytes accessed | tf_op | source)
XLA Modules:
  0.0 88.1 jit_solution(13403288469933358818)
XLA Ops:
  1.3 82.1 %shard_map.111 = (bf16[8,8192]{1,0:T(8,128)(2,1)S(1)}, bf16[1024,1536]{1,0:T(8,128)(2,1)S(1)}, bf16[1024,1536]{1,0:T(8,128)(2,1)S(1)}, bf16[1536,1024]{1,0:T(8,128)(2,1)S(1)}, s32[1]{0:T(128)}) custom-call(bf16[8,8192]{1,0:T(8,128)(2,1)} %tok_hbm.1, bf16[8,8192]{1,0:T(8,128)(2,1)} %grad_hbm.1, s32[1]{0:T(128)S(6)} %copy.28.length, bf16[1024,1536]{1,0:T(8,128)(2,1)} %gp.1, ...), custom_call_target="tpu_custom_call" | custom-call | tf_op jit(solution)/shard_map/pallas_call | solution.py:717
  83.4 0.0 copy-start.4
  83.4 0.0 copy-start.5
  83.4 3.8 %shard_map.112 = (bf16[8,8192]{1,0:T(8,128)(2,1)}, bf16[1024,1536]{1,0:T(8,128)(2,1)}, bf16[1024,1536]{1,0:T(8,128)(2,1)}, bf16[1536,1024]{1,0:T(8,128)(2,1)}) custom-call(bf16[8,8192]{1,0:T(8,128)(2,1)S(1)} %get-tuple-element.87.refs_0_, bf16[1024,1536]{1,0:T(8,128)(2,1)S(1)} %get-tuple-element.88.refs_1_, ...), custom_call_target="tpu_custom_call" | custom-call | tf_op jit(solution)/shard_map/pallas_call | solution.py:749
  87.2 0.0 copy-done.4
  87.2 0.0 copy-done.5
  87.2 0.7 while.15
Async XLA Ops:
  83.4 3.8 %copy-start.4 = (bf16[8,8192]{1,0:T(8,128)(2,1)S(1)}, bf16[8,8192]{1,0:T(8,128)(2,1)}, u32[]{:S(2)}) copy-start(bf16[8,8192]{1,0:T(8,128)(2,1)} %tok_hbm.1) | copy-start | bytes 393220
  83.4 3.8 %copy-start.5 = (bf16[8,8192]{1,0:T(8,128)(2,1)S(1)}, bf16[8,8192]{1,0:T(8,128)(2,1)}, u32[]{:S(2)}) copy-start(bf16[8,8192]{1,0:T(8,128)(2,1)} %grad_hbm.1) | copy-start | bytes 393220
